TPU v7x, 32 devices: a whole 2x2x4 slice. The times are simulated.
32 devices in a mesh: group: 2 (over x), seq: 16 (over z, y, core).
Axes of the slice: x: 2, y: 2, z: 4, core: 2. Of those that a mesh axis runs over, the one named last changes fastest.
Arguments:
- queries: bfloat16 [8192, 2048], P(('group', 'seq')), parts along dimension 0, may hold values from -9 to 9
- keys: bfloat16 [8192, 2048], P(('group', 'seq')), parts along dimension 0, may hold values from -9 to 9
- values: bfloat16 [8192, 2048], P(('group', 'seq')), parts along dimension 0, may hold values from -6 to 6
- query_dir: bfloat16 [8192, 2048], P(('group', 'seq')), parts along dimension 0, may hold values from -6 to 6
- key_dir: bfloat16 [8192, 2048], P(('group', 'seq')), parts along dimension 0, may hold values from -6 to 6
- value_dir: bfloat16 [8192, 2048], P(('group', 'seq')), parts along dimension 0, may hold values from -6 to 6
- window_width: int32 [32], P('group'), parts along dimension 0, may hold values from 0 to 2, as said below
- global_blocks: int32 [32, 2], P('group'), parts along dimension 0, may hold values from 0 to 63
- random_blocks: int32 [32, 64, 2], P('group'), parts along dimension 0, may hold values from 0 to 63
Outputs:
- query_gn: bfloat16 [8192, 2048], P(('group', 'seq')), parts along dimension 0
- key_gn: bfloat16 [8192, 2048], P(('group', 'seq')), parts along dimension 0
- value_gn: bfloat16 [8192, 2048], P(('group', 'seq')), parts along dimension 0
There are 2 independent parts, one for each index of `group`. A program takes and returns all parts, laid end to end along the dimension named above; each array names one. Nothing has to cross between parts.
Inputs may be any that keep to these rules, and one draw needn't show every extreme that they name: `window_width`: the values 0 and 2 both occur.
All inputs are finite; a program needn't handle non-finite values.
Results may differ from a plain program's by a relative error of at most 0.013.
Values may be sent and summed in bfloat16 or wider, within the bound.
A program may use at most 128 MiB of HBM per device.

v0:
```python
import functools
import math

import jax
import jax.numpy as jnp
from jax import lax
from jax.experimental import pallas as pl
from jax.experimental.pallas import tpu as pltpu
from jax.sharding import PartitionSpec as P

BLOCK = 64
WMAX = 2
PAIR = 2 * BLOCK
neg_fill = -1e30
f32 = jnp.float32
bf16 = jnp.bfloat16


def dot(lhs, rhs, lhs_dim, rhs_dim):
    return lax.dot_general(
        lhs, rhs, (((lhs_dim,), (rhs_dim,)), ((), ())), preferred_element_type=f32
    )


def attend_kernel(
    pairs, slots, live, q, dq, k, v, dk, dv, q_out, k_out, v_out, k_acc, v_acc
):
    step = pl.program_id(0)
    head_dim = q.shape[1]
    scale = 1.0 / math.sqrt(head_dim)
    slot_count = 2 * WMAX + 2 + 2 + 4
    keys = slot_count * BLOCK

    @pl.when(step == 0)
    def _():
        k_acc[...] = jnp.zeros_like(k_acc)
        v_acc[...] = jnp.zeros_like(v_acc)

    def gather(ref, starts):
        return jnp.concatenate([ref[pl.ds(start, BLOCK), :] for start in starts], axis=0)

    blank = jnp.zeros((PAIR, head_dim), bf16)
    added = []
    for pair in range(pairs):
        rows = pl.ds(pair * PAIR, PAIR)
        qb, dqb = q[rows, :], dq[rows, :]
        index = step * pairs + pair
        starts = [
            pl.multiple_of(slots[index, s] * BLOCK, BLOCK) for s in range(slot_count)
        ]
        kg, vg = gather(k, starts), gather(v, starts)
        kk = jnp.concatenate([kg, gather(dk, starts)], axis=1)
        vv = jnp.concatenate([vg, gather(dv, starts)], axis=1)
        lhs = jnp.concatenate(
            [jnp.concatenate([qb, blank], axis=1), jnp.concatenate([dqb, qb], axis=1)], axis=0
        )
        both = dot(lhs, kk, 1, 1)
        live_rows = live[pair]
        bias = jnp.concatenate(
            [jnp.broadcast_to(live_rows[h : h + 1, :], (BLOCK, keys)) for h in range(2)], axis=0
        )
        scores = jnp.where(bias > 0.5, both[:PAIR] * scale, neg_fill)
        moved = both[PAIR:] * scale
        top = jnp.max(scores, axis=1, keepdims=True)
        weights = jnp.exp(scores - top)
        weights = weights * (1.0 / jnp.sum(weights, axis=1, keepdims=True))
        mean = jnp.sum(weights * moved, axis=1, keepdims=True)
        weights_dot = weights * (moved - mean)
        wb = weights.astype(bf16)
        out = dot(jnp.concatenate([wb, weights_dot.astype(bf16)], axis=0), vv, 1, 0)
        tangent = (out[:PAIR, head_dim:] + out[PAIR:, :head_dim]).astype(bf16)
        pulled = dot(tangent, vg, 1, 1)
        centre = jnp.sum(weights * pulled, axis=1, keepdims=True)
        ds = (weights * (pulled - centre) * scale).astype(bf16)
        q_out[rows, :] = dot(ds, kg, 1, 0).astype(q_out.dtype)
        rhs = jnp.concatenate(
            [jnp.concatenate([qb, blank], axis=1), jnp.concatenate([blank, tangent], axis=1)],
            axis=0,
        )
        added.append((starts, dot(jnp.concatenate([ds, wb], axis=0), rhs, 0, 0)))
    for starts, part in added:
        for s, start in enumerate(starts):
            rows = pl.ds(start, BLOCK)
            piece = slice(s * BLOCK, (s + 1) * BLOCK)
            k_acc[rows, :] += part[piece, :head_dim]
            v_acc[rows, :] += part[piece, head_dim:]

    @pl.when(step == pl.num_programs(0) - 1)
    def _():
        k_out[...] = k_acc[...].astype(k_out.dtype)
        v_out[...] = v_acc[...].astype(v_out.dtype)


def pair_slots(first_ids, head_window, head_globals, head_randoms, block_count):
    count = first_ids.shape[0]
    offsets = jnp.arange(-WMAX, WMAX + 2, dtype=jnp.int32)
    named = first_ids[:, None] + offsets[None, :]
    inside = (named >= 0) & (named < block_count)
    halves = [
        inside & (jnp.abs(offsets - half)[None, :] <= head_window) for half in range(2)
    ]
    ones = jnp.ones((count, 2), bool)
    none = jnp.zeros((count, 2), bool)
    ids = jnp.concatenate(
        [
            jnp.clip(named, 0, block_count - 1),
            jnp.broadcast_to(head_globals[None, :], (count, 2)),
            head_randoms[first_ids],
            head_randoms[first_ids + 1],
        ],
        axis=1,
    )
    live = jnp.stack(
        [
            jnp.concatenate([halves[0], ones, ones, none], axis=1),
            jnp.concatenate([halves[1], ones, none, ones], axis=1),
        ],
        axis=1,
    )
    return ids, jnp.repeat(live.astype(f32), BLOCK, axis=2)


def head_product(rows, slots, live):
    q, k, v, dq, dk, dv = rows
    query_count, head_dim = q.shape
    tokens = k.shape[0]
    pairs = 2
    while query_count % (pairs * PAIR):
        pairs -= 1
    step_rows = pairs * PAIR
    whole = pl.BlockSpec((tokens, head_dim), lambda i, *_: (0, 0))
    part = pl.BlockSpec((step_rows, head_dim), lambda i, *_: (i, 0))
    like = lambda n: jax.ShapeDtypeStruct((n, head_dim), bf16)
    return pl.pallas_call(
        functools.partial(attend_kernel, pairs),
        grid_spec=pltpu.PrefetchScalarGridSpec(
            num_scalar_prefetch=1,
            grid=(query_count // step_rows,),
            in_specs=[
                pl.BlockSpec((pairs,) + live.shape[1:], lambda i, *_: (i, 0, 0)),
                part,
                part,
                whole,
                whole,
                whole,
                whole,
            ],
            out_specs=[part, whole, whole],
            scratch_shapes=[
                pltpu.VMEM((tokens, head_dim), f32),
                pltpu.VMEM((tokens, head_dim), f32),
            ],
        ),
        out_shape=[like(query_count), like(tokens), like(tokens)],
        compiler_params=pltpu.CompilerParams(
            dimension_semantics=("arbitrary",), vmem_limit_bytes=56 * 1024 * 1024
        ),
    )(slots, live, q, dq, k, v, dk, dv)


def shards(
    queries, keys, values, query_dir, key_dir, value_dir, window_width, global_blocks, random_blocks
):
    devices = lax.axis_size("seq")
    head_count = window_width.shape[0]
    group_size = devices // head_count
    device_index = lax.axis_index("seq")
    head_id = device_index // group_size
    residue = device_index % group_size
    tokens, features = queries.shape
    head_dim = features // head_count
    local_blocks = tokens // BLOCK
    own_blocks = local_blocks // group_size
    own = own_blocks * BLOCK
    block_count = local_blocks * devices

    def swap(array):
        return lax.all_to_all(array, "seq", split_axis=0, concat_axis=0, tiled=True)

    def to_owner(array):
        array = array.reshape(group_size, own, head_count, head_dim).transpose(2, 0, 1, 3)
        return swap(array.reshape(devices * own, head_dim))

    def to_every(array):
        array = array.reshape(tokens, head_count, head_dim).transpose(1, 0, 2)
        array = jnp.broadcast_to(array[:, None], (head_count, group_size, tokens, head_dim))
        return swap(array.reshape(devices * tokens, head_dim))

    rows = [
        to_owner(queries),
        to_every(keys),
        to_every(values),
        to_owner(query_dir),
        to_every(key_dir),
        to_every(value_dir),
    ]
    counter = 2 * jnp.arange(devices * own_blocks // 2, dtype=jnp.int32)
    first_ids = counter // own_blocks * local_blocks + residue * own_blocks + counter % own_blocks
    slots, live = pair_slots(
        first_ids,
        window_width[head_id],
        global_blocks[head_id],
        random_blocks[head_id],
        block_count,
    )
    query_grad, key_grad, value_grad = head_product(rows, slots, live)
    query_gn = (
        swap(query_grad)
        .reshape(head_count, group_size, own, head_dim)
        .transpose(1, 2, 0, 3)
        .reshape(tokens, features)
    )

    def owner_sum(array):
        array = swap(array).reshape(head_count, group_size, tokens, head_dim)
        array = array[:, 0] if group_size == 1 else array.astype(f32).sum(axis=1).astype(bf16)
        return array.transpose(1, 0, 2).reshape(tokens, features)

    return (query_gn, owner_sum(key_grad), owner_sum(value_grad))


def solution(mesh):
    rows = P(("group", "seq"), None)
    placed = (rows,) * 6 + (P("group"), P("group", None), P("group", None, None))
    return jax.shard_map(
        shards, mesh=mesh, in_specs=placed, out_specs=(rows,) * 3, check_vma=False
    )
```

profile of v0, /device:TPU:9, one launch (start us, length us, event | category | flops | bytes accessed | tf_op | source)
XLA Modules:
  0.0 327.8 jit_solution(7480988993616886012)
XLA Ops:
  0.6 1.5 copy.59
  2.2 1.2 copy.73
  3.4 6.6 %all-to-all-start = ((bf16[16,256,128]{2,1,0:T(8,128)(2,1)}), bf16[16,256,128]{2,1,0:T(8,128)(2,1)S(1)}, u32[]{:S(2)}, u32[]{:S(2)}) async-start(bf16[16,256,128]{2,1,0:T(8,128)(2,1)} %bitcast.85), calls=%async_computation | async-start | bytes 2097152 | tf_op jit(solution)/shard_map/all_to_all | solution.py:178
  10.1 1.2 bitcast_bitcast_fusion.3
  11.3 23.6 %all-to-all-done = bf16[16,256,128]{2,1,0:T(8,128)(2,1)S(1)} async-done(((bf16[16,256,128]{2,1,0:T(8,128)(2,1)}), bf16[16,256,128]{2,1,0:T(8,128)(2,1)S(1)}, u32[]{:S(2)}, u32[]{:S(2)}) %all-to-all-start) | async-done | bytes 1048608 | tf_op jit(solution)/shard_map/all_to_all | solution.py:178
  34.9 5.0 %all-to-all-start.2 = ((bf16[16,256,128]{2,1,0:T(8,128)(2,1)}), bf16[16,256,128]{2,1,0:T(8,128)(2,1)S(1)}, u32[]{:S(2)}, u32[]{:S(2)}) async-start(bf16[16,256,128]{2,1,0:T(8,128)(2,1)} %bitcast_bitcast_fusion.3), calls=%async_computation.2 | async-start | bytes 2097152 | tf_op jit(solution)/shard_map/all_to_all | solution.py:178
  39.9 2.5 bitcast_bitcast_fusion.2
  42.4 22.3 %all-to-all-done.2 = bf16[16,256,128]{2,1,0:T(8,128)(2,1)S(1)} async-done(((bf16[16,256,128]{2,1,0:T(8,128)(2,1)}), bf16[16,256,128]{2,1,0:T(8,128)(2,1)S(1)}, u32[]{:S(2)}, u32[]{:S(2)}) %all-to-all-start.2) | async-done | bytes 1048608 | tf_op jit(solution)/shard_map/all_to_all | solution.py:178
  64.7 5.0 %all-to-all-start.3 = ((bf16[16,256,128]{2,1,0:T(8,128)(2,1)}), bf16[16,256,128]{2,1,0:T(8,128)(2,1)S(1)}, u32[]{:S(2)}, u32[]{:S(2)}) async-start(bf16[16,256,128]{2,1,0:T(8,128)(2,1)} %bitcast_bitcast_fusion.2), calls=%async_computation.3 | async-start | bytes 2097152 | tf_op jit(solution)/shard_map/all_to_all | solution.py:178
  69.7 1.5 copy.60
  71.1 1.2 copy.72
  72.4 22.1 %all-to-all-done.3 = bf16[16,256,128]{2,1,0:T(8,128)(2,1)S(1)} async-done(((bf16[16,256,128]{2,1,0:T(8,128)(2,1)}), bf16[16,256,128]{2,1,0:T(8,128)(2,1)S(1)}, u32[]{:S(2)}, u32[]{:S(2)}) %all-to-all-start.3) | async-done | bytes 1048608 | tf_op jit(solution)/shard_map/all_to_all | solution.py:178
  94.5 1.0 copy-done.3
  95.5 5.0 %all-to-all-start.1 = ((bf16[16,256,128]{2,1,0:T(8,128)(2,1)}), bf16[16,256,128]{2,1,0:T(8,128)(2,1)S(1)}, u32[]{:S(2)}, u32[]{:S(2)}) async-start(bf16[16,256,128]{2,1,0:T(8,128)(2,1)} %bitcast.92), calls=%async_computation.1 | async-start | bytes 2097152 | tf_op jit(solution)/shard_map/all_to_all | solution.py:178
  100.5 2.5 bitcast_bitcast_fusion.1
  103.0 22.4 %all-to-all-done.1 = bf16[16,256,128]{2,1,0:T(8,128)(2,1)S(1)} async-done(((bf16[16,256,128]{2,1,0:T(8,128)(2,1)}), bf16[16,256,128]{2,1,0:T(8,128)(2,1)S(1)}, u32[]{:S(2)}, u32[]{:S(2)}) %all-to-all-start.1) | async-done | bytes 1048608 | tf_op jit(solution)/shard_map/all_to_all | solution.py:178
  125.4 1.0 copy-done.4
  126.3 5.0 %all-to-all-start.4 = ((bf16[16,256,128]{2,1,0:T(8,128)(2,1)}), bf16[16,256,128]{2,1,0:T(8,128)(2,1)S(1)}, u32[]{:S(2)}, u32[]{:S(2)}) async-start(bf16[16,256,128]{2,1,0:T(8,128)(2,1)} %bitcast_bitcast_fusion.1), calls=%async_computation.4 | async-start | bytes 2097152 | tf_op jit(solution)/shard_map/all_to_all | solution.py:178
  131.3 2.5 bitcast_bitcast_fusion
  133.8 22.4 %all-to-all-done.4 = bf16[16,256,128]{2,1,0:T(8,128)(2,1)S(1)} async-done(((bf16[16,256,128]{2,1,0:T(8,128)(2,1)}), bf16[16,256,128]{2,1,0:T(8,128)(2,1)S(1)}, u32[]{:S(2)}, u32[]{:S(2)}) %all-to-all-start.4) | async-done | bytes 1048608 | tf_op jit(solution)/shard_map/all_to_all | solution.py:178
  156.1 5.0 %all-to-all-start.5 = ((bf16[16,256,128]{2,1,0:T(8,128)(2,1)}), bf16[16,256,128]{2,1,0:T(8,128)(2,1)S(1)}, u32[]{:S(2)}, u32[]{:S(2)}) async-start(bf16[16,256,128]{2,1,0:T(8,128)(2,1)} %bitcast_bitcast_fusion), calls=%async_computation.5 | async-start | bytes 2097152 | tf_op jit(solution)/shard_map/all_to_all | solution.py:178
  167.6 18.4 %all-to-all-done.5 = bf16[16,256,128]{2,1,0:T(8,128)(2,1)S(1)} async-done(((bf16[16,256,128]{2,1,0:T(8,128)(2,1)}), bf16[16,256,128]{2,1,0:T(8,128)(2,1)S(1)}, u32[]{:S(2)}, u32[]{:S(2)}) %all-to-all-start.5) | async-done | bytes 1048608 | tf_op jit(solution)/shard_map/all_to_all | solution.py:178
  186.0 1.0 copy-done.6
  186.9 50.2 %shard_map.112 = (bf16[4096,128]{1,0:T(8,128)(2,1)}, bf16[4096,128]{1,0:T(8,128)(2,1)}, bf16[4096,128]{1,0:T(8,128)(2,1)}) custom-call(s32[32,12]{1,0:T(8,128)} %pad_add_fusion.slots, f32[32,2,768]{2,1,0:T(2,128)} %copy.46.live, bf16[4096,128]{1,0:T(8,128)(2,1)} %bitcast.86, bf16[4096,128]{1,0:T(8,128)(2,1)} %bitcast.89, bf16[4096,128]{1,0:T(8,128)(2,1)} %bitcast.87, ...), custom_call_target="tpu_custom_call" | custom-call | tf_op jit(solution)/shard_map/pallas_call | solution.py:134
  237.1 30.5 %all_to_all.81 = bf16[16,256,128]{2,1,0:T(8,128)(2,1)S(1)} all-to-all(bf16[16,256,128]{2,1,0:T(8,128)(2,1)} %bitcast.102), channel_id=1, replica_groups=mesh['group'=2,'seq'=16] {'seq'}, dimensions={0} | all-to-all | bytes 2097152 | tf_op jit(solution)/shard_map/all_to_all | solution.py:178
  267.6 29.7 %all_to_all.82 = bf16[16,256,128]{2,1,0:T(8,128)(2,1)} all-to-all(bf16[16,256,128]{2,1,0:T(8,128)(2,1)S(1)} %bitcast.101), channel_id=1, replica_groups=mesh['group'=2,'seq'=16] {'seq'}, dimensions={0} | all-to-all | bytes 2097152 | tf_op jit(solution)/shard_map/all_to_all | solution.py:178
  297.4 4.5 %all-to-all-start.8 = ((bf16[16,256,128]{2,1,0:T(8,128)(2,1)}), bf16[16,256,128]{2,1,0:T(8,128)(2,1)S(1)}, u32[]{:S(2)}, u32[]{:S(2)}) async-start(bf16[16,256,128]{2,1,0:T(8,128)(2,1)} %bitcast.99), calls=%async_computation.8 | async-start | bytes 2097152 | tf_op jit(solution)/shard_map/all_to_all | solution.py:178
  301.8 1.9 copy.47
  303.7 1.2 copy.71
  305.0 1.1 copy_bitcast_fusion.2
  306.1 20.6 %all-to-all-done.8 = bf16[16,256,128]{2,1,0:T(8,128)(2,1)S(1)} async-done(((bf16[16,256,128]{2,1,0:T(8,128)(2,1)}), bf16[16,256,128]{2,1,0:T(8,128)(2,1)S(1)}, u32[]{:S(2)}, u32[]{:S(2)}) %all-to-all-start.8) | async-done | bytes 1048608 | tf_op jit(solution)/shard_map/all_to_all | solution.py:178
  326.7 1.1 copy_bitcast_fusion.1
  (42 shorter events, 6.4 us)
Async XLA Ops:
  0.6 9.4 %copy-start = (bf16[256,2048]{1,0:T(8,128)(2,1)S(1)}, bf16[256,2048]{1,0:T(8,128)(2,1)}, u32[]{:S(2)}) copy-start(bf16[256,2048]{1,0:T(8,128)(2,1)} %param.10) | copy-start | bytes 3145732
  3.4 31.5 %all-to-all-start = ((bf16[16,256,128]{2,1,0:T(8,128)(2,1)}), bf16[16,256,128]{2,1,0:T(8,128)(2,1)S(1)}, u32[]{:S(2)}, u32[]{:S(2)}) async-start(bf16[16,256,128]{2,1,0:T(8,128)(2,1)} %bitcast.85), calls=%async_computation | async-start | bytes 2097152 | tf_op jit(solution)/shard_map/all_to_all | solution.py:178
  34.9 7.5 %copy-start.1 = (bf16[16,256,128]{2,1,0:T(8,128)(2,1)}, bf16[16,256,128]{2,1,0:T(8,128)(2,1)S(1)}, u32[]{:S(2)}) copy-start(bf16[16,256,128]{2,1,0:T(8,128)(2,1)S(1)} %all-to-all-done) | copy-start | bytes 3145732
  34.9 29.8 %all-to-all-start.2 = ((bf16[16,256,128]{2,1,0:T(8,128)(2,1)}), bf16[16,256,128]{2,1,0:T(8,128)(2,1)S(1)}, u32[]{:S(2)}, u32[]{:S(2)}) async-start(bf16[16,256,128]{2,1,0:T(8,128)(2,1)} %bitcast_bitcast_fusion.3), calls=%async_computation.2 | async-start | bytes 2097152 | tf_op jit(solution)/shard_map/all_to_all | solution.py:178
  64.7 5.0 %copy-start.2 = (bf16[16,256,128]{2,1,0:T(8,128)(2,1)}, bf16[16,256,128]{2,1,0:T(8,128)(2,1)S(1)}, u32[]{:S(2)}) copy-start(bf16[16,256,128]{2,1,0:T(8,128)(2,1)S(1)} %all-to-all-done.2) | copy-start | bytes 3145732
  64.7 29.8 %all-to-all-start.3 = ((bf16[16,256,128]{2,1,0:T(8,128)(2,1)}), bf16[16,256,128]{2,1,0:T(8,128)(2,1)S(1)}, u32[]{:S(2)}, u32[]{:S(2)}) async-start(bf16[16,256,128]{2,1,0:T(8,128)(2,1)} %bitcast_bitcast_fusion.2), calls=%async_computation.3 | async-start | bytes 2097152 | tf_op jit(solution)/shard_map/all_to_all | solution.py:178
  94.5 1.0 copy-start.3
  95.5 29.8 %all-to-all-start.1 = ((bf16[16,256,128]{2,1,0:T(8,128)(2,1)}), bf16[16,256,128]{2,1,0:T(8,128)(2,1)S(1)}, u32[]{:S(2)}, u32[]{:S(2)}) async-start(bf16[16,256,128]{2,1,0:T(8,128)(2,1)} %bitcast.92), calls=%async_computation.1 | async-start | bytes 2097152 | tf_op jit(solution)/shard_map/all_to_all | solution.py:178
  125.4 1.0 copy-start.4
  126.3 29.8 %all-to-all-start.4 = ((bf16[16,256,128]{2,1,0:T(8,128)(2,1)}), bf16[16,256,128]{2,1,0:T(8,128)(2,1)S(1)}, u32[]{:S(2)}, u32[]{:S(2)}) async-start(bf16[16,256,128]{2,1,0:T(8,128)(2,1)} %bitcast_bitcast_fusion.1), calls=%async_computation.4 | async-start | bytes 2097152 | tf_op jit(solution)/shard_map/all_to_all | solution.py:178
  156.1 5.0 %copy-start.5 = (bf16[16,256,128]{2,1,0:T(8,128)(2,1)}, bf16[16,256,128]{2,1,0:T(8,128)(2,1)S(1)}, u32[]{:S(2)}) copy-start(bf16[16,256,128]{2,1,0:T(8,128)(2,1)S(1)} %all-to-all-done.4) | copy-start | bytes 3145732
  156.1 29.8 %all-to-all-start.5 = ((bf16[16,256,128]{2,1,0:T(8,128)(2,1)}), bf16[16,256,128]{2,1,0:T(8,128)(2,1)S(1)}, u32[]{:S(2)}, u32[]{:S(2)}) async-start(bf16[16,256,128]{2,1,0:T(8,128)(2,1)} %bitcast_bitcast_fusion), calls=%async_computation.5 | async-start | bytes 2097152 | tf_op jit(solution)/shard_map/all_to_all | solution.py:178
  161.1 0.7 copy-start.9
  161.8 0.7 copy-start.8
  186.0 1.0 copy-start.6
  237.1 30.5 %copy-start.7 = (bf16[4096,128]{1,0:T(8,128)(2,1)S(1)}, bf16[4096,128]{1,0:T(8,128)(2,1)}, u32[]{:S(2)}) copy-start(bf16[4096,128]{1,0:T(8,128)(2,1)} %get-tuple-element.6) | copy-start | bytes 3145732
  297.4 29.3 %all-to-all-start.8 = ((bf16[16,256,128]{2,1,0:T(8,128)(2,1)}), bf16[16,256,128]{2,1,0:T(8,128)(2,1)S(1)}, u32[]{:S(2)}, u32[]{:S(2)}) async-start(bf16[16,256,128]{2,1,0:T(8,128)(2,1)} %bitcast.99), calls=%async_computation.8 | async-start | bytes 2097152 | tf_op jit(solution)/shard_map/all_to_all | solution.py:178
where the time goes:
time: 329 us; the launch traced here: 328 us
  waiting for transfers between devices  152 us (46%)
  blocking collectives  60.2 us (18%)
  Pallas kernels  50.2 us (15%)
  starting transfers between devices  35.9 us (11%)
  local copies, waits for them, and re-layouts  27.3 us (8%)
    all_to_all x7, waiting for transfers between devices, swap(): return lax.all_to_all(array, 'seq', split_axis=0, concat_axis=0, tiled=True)  152 us
    all_to_all x2, blocking collectives, swap(): return lax.all_to_all(array, 'seq', split_axis=0, concat_axis=0, tiled=True)  60.2 us
    pallas_call x1, Pallas kernels, head_product(): pl.pallas_call(functools.partial(attend_kernel, pairs), grid_spec=pltpu.P...  50.2 us
    all_to_all x7, starting transfers between devices, swap(): return lax.all_to_all(array, 'seq', split_axis=0, concat_axis=0, tiled=True)  35.9 us
    transpose x4, local copies, waits for them, and re-layouts, to_every(): array = array.reshape(tokens, head_count, head_dim).transpose(1, 0, 2)  8.69 us
    unnamed x23, local copies, waits for them, and re-layouts  7.93 us
  transfers between devices with their start and end apart: 7, of which 7 were waited for; matrix products, arithmetic and copies ran while one was open for 7% of the time, Pallas kernels for 0%

commit v1 on v0

v1 whole, which is shorter than its diff:
```python
import functools
import math

import jax
import jax.numpy as jnp
from jax import lax
from jax.experimental import pallas as pl
from jax.experimental.pallas import tpu as pltpu
from jax.sharding import PartitionSpec as P

BLOCK = 64
WMAX = 2
PAIR = 2 * BLOCK
SLOTS = 2 * WMAX + 2 + 2 + 4
STRIDE = 7
MESH = pl.DeviceIdType.MESH
neg_fill = -1e30
f32 = jnp.float32
bf16 = jnp.bfloat16


def dot(lhs, rhs, lhs_dim, rhs_dim):
    return lax.dot_general(
        lhs, rhs, (((lhs_dim,), (rhs_dim,)), ((), ())), preferred_element_type=f32
    )


def pair_product(qb, dqb, kg, vg, dkg, dvg, live_rows):
    head_dim = qb.shape[1]
    scale = 1.0 / math.sqrt(head_dim)
    blank = jnp.zeros((PAIR, head_dim), bf16)
    kk = jnp.concatenate([kg, dkg], axis=1)
    vv = jnp.concatenate([vg, dvg], axis=1)
    first = jnp.concatenate([qb, blank], axis=1)
    lhs = jnp.concatenate([first, jnp.concatenate([dqb, qb], axis=1)], axis=0)
    both = dot(lhs, kk, 1, 1)
    bias = jnp.concatenate(
        [jnp.broadcast_to(live_rows[h : h + 1, :], (BLOCK, SLOTS * BLOCK)) for h in range(2)],
        axis=0,
    )
    scores = jnp.where(bias > 0.5, both[:PAIR] * scale, neg_fill)
    moved = both[PAIR:] * scale
    top = jnp.max(scores, axis=1, keepdims=True)
    weights = jnp.exp(scores - top)
    weights = weights * (1.0 / jnp.sum(weights, axis=1, keepdims=True))
    mean = jnp.sum(weights * moved, axis=1, keepdims=True)
    wb = weights.astype(bf16)
    weights_dot = (weights * (moved - mean)).astype(bf16)
    out = dot(jnp.concatenate([wb, weights_dot], axis=0), vv, 1, 0)
    tangent = (out[:PAIR, head_dim:] + out[PAIR:, :head_dim]).astype(bf16)
    pulled = dot(tangent, vg, 1, 1)
    centre = jnp.sum(weights * pulled, axis=1, keepdims=True)
    ds = (weights * (pulled - centre) * scale).astype(bf16)
    query_part = dot(ds, kg, 1, 0).astype(bf16)
    rhs = jnp.concatenate([first, jnp.concatenate([blank, tangent], axis=1)], axis=0)
    return query_part, dot(jnp.concatenate([ds, wb], axis=0), rhs, 0, 0)


def greet(me, devices):
    barrier = pltpu.get_barrier_semaphore()
    for step in range(1, devices):
        pl.semaphore_signal(
            barrier, inc=1, device_id={"seq": lax.rem(me + step, devices)}, device_id_type=MESH
        )
    pl.semaphore_wait(barrier, devices - 1)


def columns(head, head_dim):
    return pl.ds(pl.multiple_of(head * head_dim, head_dim), head_dim)


def rows_at(index, count):
    return pl.ds(pl.multiple_of(index * count, count), count)


def main_kernel(
    devices, group_size,
    slots, live, q, k, v, dq, dk, dv,
    q_gn, window, fixed, drawn,
    q_all, k_all, v_all, dq_all, dk_all, dv_all, q_res,
    send, recv, q_send, q_recv,
):
    me = lax.axis_index("seq")
    local_blocks = k.shape[0]
    tokens = local_blocks * BLOCK
    head_dim = k_all.shape[2]
    own = tokens // group_size
    pairs = own // PAIR
    head, residue = me // group_size, lax.rem(me, group_size)
    kinds = [(k, k_all), (dk, dk_all), (v, v_all), (dv, dv_all), (q, q_all), (dq, dq_all)]
    greet(me, devices)

    def copy(kind, step):
        source, target = kinds[kind]
        to = lax.rem(me + (devices - step * STRIDE % devices), devices)
        if kind < 4:
            part = source.at[:, :, columns(to // group_size, head_dim)]
            spot = target.at[rows_at(me, local_blocks)]
        else:
            part = source.at[
                rows_at(lax.rem(to, group_size), own), columns(to // group_size, head_dim)
            ]
            spot = target.at[rows_at(me, own), :]
        if step == 0:
            return pltpu.make_async_copy(part, spot, recv.at[kind, 0])
        return pltpu.make_async_remote_copy(
            src_ref=part,
            dst_ref=spot,
            send_sem=send.at[kind, step],
            recv_sem=recv.at[kind, step],
            device_id={"seq": to},
            device_id_type=MESH,
        )

    for kind in range(6):
        for step in range(devices):
            copy(kind, step).start()
    window[...] = jnp.zeros_like(window)
    fixed[...] = jnp.zeros_like(fixed)
    for kind in range(4):
        for step in range(devices):
            if step == 0:
                copy(kind, step).wait()
            else:
                copy(kind, step).wait_recv()

    def gather(ref, ids):
        return jnp.concatenate([ref[i] for i in ids], axis=0)

    def back(step, origin):
        part = q_res.at[rows_at(origin, own), :]
        target = q_gn.at[rows_at(residue, own), columns(head, head_dim)]
        return pltpu.make_async_remote_copy(
            src_ref=part,
            dst_ref=target,
            send_sem=q_send.at[step],
            recv_sem=q_recv.at[step],
            device_id={"seq": origin},
            device_id_type=MESH,
        )

    def work(step):
        origin = lax.rem(me + step * STRIDE, devices)
        for pair in range(pairs):
            index = origin * pairs + pair
            rows = rows_at(index, PAIR)
            ids = [slots[index, s] for s in range(SLOTS)]
            query_part, added = pair_product(
                q_all[rows, :], dq_all[rows, :],
                gather(k_all, ids), gather(v_all, ids),
                gather(dk_all, ids), gather(dv_all, ids),
                live[index],
            )
            q_res[rows, :] = query_part
            first = origin * (tokens // BLOCK) + residue * (own // BLOCK) + 2 * pair
            near = (2 * WMAX + 2) * BLOCK
            spot = pl.ds(pl.multiple_of(first * BLOCK, BLOCK), near)
            window[spot, :] += added[:near]
            fixed[...] += added[near : near + PAIR]
            drawn[rows_at(index, 2 * PAIR), :] = added[near + PAIR :].astype(bf16)
        return origin

    own_copy = pltpu.make_async_copy(
        q_res.at[rows_at(me, own), :],
        q_gn.at[rows_at(residue, own), columns(head, head_dim)],
        q_recv.at[0],
    )
    copy(4, 0).wait()
    copy(5, 0).wait()
    work(0)
    own_copy.start()

    def wait_rows(kind, step):
        source, target = kinds[kind]
        pltpu.make_async_remote_copy(
            src_ref=source.at[rows_at(residue, own), columns(head, head_dim)],
            dst_ref=target.at[rows_at(lax.rem(me + step * STRIDE, devices), own), :],
            send_sem=send.at[kind, step],
            recv_sem=recv.at[kind, step],
            device_id={"seq": lax.rem(me + step * STRIDE, devices)},
            device_id_type=MESH,
        ).wait_recv()

    @pl.loop(1, devices)
    def _(step):
        wait_rows(4, step)
        wait_rows(5, step)
        origin = work(step)
        back(step, origin).start()

    for kind in range(6):
        for step in range(1, devices):
            copy(kind, step).wait_send()
    own_copy.wait()
    for step in range(1, devices):
        giver = lax.rem(me + (devices - step * STRIDE % devices), devices)
        pltpu.make_async_remote_copy(
            src_ref=q_res.at[rows_at(giver, own), :],
            dst_ref=q_gn.at[
                rows_at(lax.rem(giver, group_size), own),
                columns(giver // group_size, head_dim),
            ],
            send_sem=q_send.at[step],
            recv_sem=q_recv.at[step],
            device_id={"seq": giver},
            device_id_type=MESH,
        ).wait()


def add_kernel(slots, window, fixed, drawn, k_out, v_out, acc):
    tokens, head_dim = k_out.shape
    acc[...] = window[pl.ds(WMAX * BLOCK, tokens), :]
    for s in range(2):
        rows = rows_at(slots[0, 2 * WMAX + 2 + s], BLOCK)
        acc[rows, :] += fixed[s * BLOCK : (s + 1) * BLOCK, :]

    @pl.loop(0, slots.shape[0])
    def _(index):
        for s in range(4):
            rows = rows_at(slots[index, 2 * WMAX + 4 + s], BLOCK)
            acc[rows, :] += drawn[rows_at(index * 4 + s, BLOCK), :].astype(f32)

    k_out[...] = acc[:, :head_dim].astype(bf16)
    v_out[...] = acc[:, head_dim:].astype(bf16)


def return_kernel(devices, group_size, k, v, k_gn, v_gn, send, recv):
    me = lax.axis_index("seq")
    tokens, head_dim = k.shape[0] // devices, k.shape[1]
    greet(me, devices)

    def copy(kind, step):
        source, target = ((k, k_gn), (v, v_gn))[kind]
        to = lax.rem(me + step * STRIDE, devices)
        part = source.at[rows_at(to, tokens), :]
        spot = target.at[lax.rem(me, group_size), :, columns(me // group_size, head_dim)]
        if step == 0:
            return pltpu.make_async_copy(part, spot, recv.at[kind, 0])
        return pltpu.make_async_remote_copy(
            src_ref=part,
            dst_ref=spot,
            send_sem=send.at[kind, step],
            recv_sem=recv.at[kind, step],
            device_id={"seq": to},
            device_id_type=MESH,
        )

    for kind in range(2):
        for step in range(devices):
            copy(kind, step).start()
    for kind in range(2):
        for step in range(devices):
            copy(kind, step).wait()


def pair_slots(first_ids, head_window, head_globals, head_randoms, block_count):
    count = first_ids.shape[0]
    offsets = jnp.arange(-WMAX, WMAX + 2, dtype=jnp.int32)
    named = first_ids[:, None] + offsets[None, :]
    inside = (named >= 0) & (named < block_count)
    halves = [
        inside & (jnp.abs(offsets - half)[None, :] <= head_window) for half in range(2)
    ]
    ones = jnp.ones((count, 2), bool)
    none = jnp.zeros((count, 2), bool)
    ids = jnp.concatenate(
        [
            jnp.clip(named, 0, block_count - 1),
            jnp.broadcast_to(head_globals[None, :], (count, 2)),
            head_randoms[first_ids],
            head_randoms[first_ids + 1],
        ],
        axis=1,
    )
    live = jnp.stack(
        [
            jnp.concatenate([halves[0], ones, ones, none], axis=1),
            jnp.concatenate([halves[1], ones, none, ones], axis=1),
        ],
        axis=1,
    )
    return ids, jnp.repeat(live.astype(f32), BLOCK, axis=2)


def shards(
    queries, keys, values, query_dir, key_dir, value_dir, window_width, global_blocks, random_blocks
):
    devices = lax.axis_size("seq")
    head_count = window_width.shape[0]
    group_size = devices // head_count
    device_index = lax.axis_index("seq")
    head_id = device_index // group_size
    residue = device_index % group_size
    tokens, features = queries.shape
    head_dim = features // head_count
    local_blocks = tokens // BLOCK
    own_blocks = local_blocks // group_size
    own = own_blocks * BLOCK
    block_count = local_blocks * devices
    whole = devices * tokens
    counter = 2 * jnp.arange(devices * own_blocks // 2, dtype=jnp.int32)
    first_ids = counter // own_blocks * local_blocks + residue * own_blocks + counter % own_blocks
    slots, live = pair_slots(
        first_ids,
        window_width[head_id],
        global_blocks[head_id],
        random_blocks[head_id],
        block_count,
    )
    by_block = lambda array: array.reshape(local_blocks, BLOCK, features)
    any_spec = pl.BlockSpec(memory_space=pl.ANY)
    vmem = pl.BlockSpec(memory_space=pltpu.VMEM)
    smem = pl.BlockSpec(memory_space=pltpu.SMEM)
    limit = 56 * 1024 * 1024
    count = slots.shape[0]
    shape = jax.ShapeDtypeStruct
    rows, mine = pltpu.VMEM((block_count, BLOCK, head_dim), bf16), pltpu.VMEM((devices * own, head_dim), bf16)
    dma = pltpu.SemaphoreType.DMA
    query_gn, window, fixed, drawn = pl.pallas_call(
        functools.partial(main_kernel, devices, group_size),
        out_shape=[
            shape((tokens, features), bf16),
            shape((whole + 2 * WMAX * BLOCK, 2 * head_dim), f32),
            shape((2 * BLOCK, 2 * head_dim), f32),
            shape((count * 4 * BLOCK, 2 * head_dim), bf16),
        ],
        in_specs=[smem, vmem] + [any_spec] * 6,
        out_specs=[any_spec, vmem, vmem, vmem],
        scratch_shapes=[
            mine, rows, rows, mine, rows, rows, mine,
            dma((6, devices)), dma((6, devices)), dma((devices,)), dma((devices,)),
        ],
        compiler_params=pltpu.CompilerParams(
            collective_id=0, has_side_effects=True, vmem_limit_bytes=limit
        ),
    )(
        slots, live, queries, by_block(keys), by_block(values),
        query_dir, by_block(key_dir), by_block(value_dir),
    )
    key_grad, value_grad = pl.pallas_call(
        add_kernel,
        out_shape=[shape((whole, head_dim), bf16)] * 2,
        in_specs=[smem, vmem, vmem, vmem],
        out_specs=[vmem, vmem],
        scratch_shapes=[pltpu.VMEM((whole, 2 * head_dim), f32)],
        compiler_params=pltpu.CompilerParams(vmem_limit_bytes=limit),
    )(slots, window, fixed, drawn)
    key_gn, value_gn = pl.pallas_call(
        functools.partial(return_kernel, devices, group_size),
        out_shape=[shape((group_size, tokens, features), bf16)] * 2,
        in_specs=[any_spec] * 2,
        out_specs=[any_spec] * 2,
        scratch_shapes=[dma((2, devices)), dma((2, devices))],
        compiler_params=pltpu.CompilerParams(collective_id=1, has_side_effects=True),
    )(key_grad, value_grad)

    def owner_sum(array):
        return array[0] if group_size == 1 else array.astype(f32).sum(axis=0).astype(bf16)

    return (query_gn, owner_sum(key_gn), owner_sum(value_gn))


def solution(mesh):
    rows = P(("group", "seq"), None)
    placed = (rows,) * 6 + (P("group"), P("group", None), P("group", None, None))
    return jax.shard_map(
        shards, mesh=mesh, in_specs=placed, out_specs=(rows,) * 3, check_vma=False
    )
```

time: 329 us -> 254 us (0.77)
  Pallas kernels: 50.2 us -> 240 us
  waiting for transfers between devices: 152 us -> 0 us
  blocking collectives: 60.2 us -> 0 us
  starting transfers between devices: 35.9 us -> 0 us
  local copies, waits for them, and re-layouts: 27.3 us -> 8.94 us
    pallas_call x1 -> x3, Pallas kernels: 50.2 us -> 240 us  [the longest x1 180 us: shards(): pl.pallas_call(functools.partial(main_kernel, devices, group_size), out_s...]
    all_to_all x7 -> x0, waiting for transfers between devices: 152 us -> none  [swap(): return lax.all_to_all(array, 'seq', split_axis=0, concat_axis=0, tiled=True)]
    all_to_all x2 -> x0, blocking collectives: 60.2 us -> none  [swap(): return lax.all_to_all(array, 'seq', split_axis=0, concat_axis=0, tiled=True)]
    all_to_all x7 -> x0, starting transfers between devices: 35.9 us -> none  [swap(): return lax.all_to_all(array, 'seq', split_axis=0, concat_axis=0, tiled=True)]
    transpose x5 -> x0, local copies, waits for them, and re-layouts: 10.6 us -> none  [the longest x4 8.69 us: to_every(): array = array.reshape(tokens, head_count, head_dim).transpose(1, 0, 2)]
    reshape x4 -> x0, local copies, waits for them, and re-layouts: 4.75 us -> none  [the longest x2 2.49 us: to_owner(): array.reshape(group_size, own, head_count, head_dim).transpose(2, 0, 1, 3)]
    unnamed x23 -> x9, local copies, waits for them, and re-layouts: 7.93 us -> 4.26 us
  transfers between devices with their start and end apart: 7 -> 0, of which waited for: 7 -> 0; matrix products, arithmetic and copies ran while one was open for 7% -> 0% of each run, Pallas kernels for 0% -> 0%
where the time goes in v1:
time: 254 us; the launch traced here: 251 us
  Pallas kernels  240 us (94%)
  local copies, waits for them, and re-layouts  8.94 us (4%)
    pallas_call x1, Pallas kernels, shards(): pl.pallas_call(functools.partial(main_kernel, devices, group_size), out_s...  180 us
    pallas_call x1, Pallas kernels, shards(): pl.pallas_call(functools.partial(return_kernel, devices, group_size), out...  53.3 us
    pallas_call x1, Pallas kernels, shards(): pl.pallas_call(add_kernel, out_shape=[shape((whole, head_dim), bf16)] * 2...  6.47 us

profile of v1, /device:TPU:9, one launch (start us, length us, event | category | flops | bytes accessed | tf_op | source)
XLA Modules:
  0.0 251.2 jit_solution(3633761384240121243)
XLA Ops:
  0.6 0.0 copy-start
  0.6 1.2 dynamic_slice.11
  1.9 0.9 dynamic-slice_reduce_fusion
  2.8 0.1 pad.10.clone
  2.9 0.0 copy-done
  2.9 0.1 pad.7.clone
  2.9 0.7 abs_compare_fusion
  3.6 0.1 fusion.2
  3.8 0.1 add_bitcast_fusion
  3.8 0.1 add_clamp_fusion
  3.9 0.1 copy.19
  4.0 0.6 gather_fusion.1
  4.6 0.6 gather_fusion
  5.2 0.7 pad_add_fusion.slots
  5.9 0.2 broadcast_in_dim.26
  6.1 0.1 reshape.138
  6.2 0.8 copy.22.live
  7.0 180.1 %shard_map.112 = (bf16[256,2048]{1,0:T(8,128)(2,1)}, f32[4352,256]{1,0:T(8,128)}, f32[128,256]{1,0:T(8,128)}, bf16[8192,256]{1,0:T(8,128)(2,1)}) custom-call(s32[32,12]{1,0:T(8,128)} %pad_add_fusion.slots, f32[32,2,768]{2,1,0:T(2,128)} %copy.22.live, bf16[256,2048]{1,0:T(8,128)(2,1)} %q.1, bf16[4,64,2048]{2,1,0:T(8,128)(2,1)} %bitcast.19, ...), custom_call_target="tpu_custom_call" | custom-call | tf_op jit(solution)/shard_map/pallas_call | solution.py:319
  187.1 0.0 copy-start.1
  187.2 6.5 %shard_map.113 = (bf16[4096,128]{1,0:T(8,128)(2,1)}, bf16[4096,128]{1,0:T(8,128)(2,1)}) custom-call(s32[32,12]{1,0:T(8,128)} %pad_add_fusion.slots, f32[4352,256]{1,0:T(8,128)} %get-tuple-element.12.window, f32[128,256]{1,0:T(8,128)} %get-tuple-element.13.fixed, bf16[8192,256]{1,0:T(8,128)(2,1)} %get-tuple-element.14.drawn), custom_call_target="tpu_custom_call" | custom-call | tf_op jit(solution)/shard_map/pallas_call | solution.py:340
  193.6 53.3 %shard_map.114 = (bf16[1,256,2048]{2,1,0:T(8,128)(2,1)}, bf16[1,256,2048]{2,1,0:T(8,128)(2,1)}) custom-call(bf16[4096,128]{1,0:T(8,128)(2,1)} %get-tuple-element.15.k, bf16[4096,128]{1,0:T(8,128)(2,1)} %get-tuple-element.16.v), custom_call_target="tpu_custom_call" | custom-call | tf_op jit(solution)/shard_map/pallas_call | solution.py:348
  247.0 0.0 copy-start.2
  247.0 0.0 copy-done.1
  247.0 1.0 copy.29
  248.0 2.3 copy.30
  250.3 0.0 copy-done.2
  250.3 1.0 copy.31
  (10 shorter events, 0.1 us)
Async XLA Ops:
  0.6 2.2 copy-start
  187.1 59.8 %copy-start.1 = (bf16[256,2048]{1,0:T(8,128)(2,1)S(1)}, bf16[256,2048]{1,0:T(8,128)(2,1)}, u32[]{:S(2)}) copy-start(bf16[256,2048]{1,0:T(8,128)(2,1)} %get-tuple-element.30) | copy-start | bytes 3145732
  247.0 3.3 %copy-start.2 = (bf16[1,256,2048]{2,1,0:T(8,128)(2,1)S(1)}, bf16[1,256,2048]{2,1,0:T(8,128)(2,1)}, u32[]{:S(2)}) copy-start(bf16[1,256,2048]{2,1,0:T(8,128)(2,1)} %get-tuple-element.18) | copy-start | bytes 3145732

commit v2 on v1

--- a/solution.py
+++ b/solution.py
@@ -12,7 +12,7 @@
 WMAX = 2
 PAIR = 2 * BLOCK
 SLOTS = 2 * WMAX + 2 + 2 + 4
-STRIDE = 7
+FLIGHT = 3
 MESH = pl.DeviceIdType.MESH
 neg_fill = -1e30
 f32 = jnp.float32
@@ -35,8 +35,7 @@
     lhs = jnp.concatenate([first, jnp.concatenate([dqb, qb], axis=1)], axis=0)
     both = dot(lhs, kk, 1, 1)
     bias = jnp.concatenate(
-        [jnp.broadcast_to(live_rows[h : h + 1, :], (BLOCK, SLOTS * BLOCK)) for h in range(2)],
-        axis=0,
+        [jnp.broadcast_to(row, (BLOCK, SLOTS * BLOCK)) for row in live_rows], axis=0
     )
     scores = jnp.where(bias > 0.5, both[:PAIR] * scale, neg_fill)
     moved = both[PAIR:] * scale
@@ -56,6 +55,21 @@
     return query_part, dot(jnp.concatenate([ds, wb], axis=0), rhs, 0, 0)
 
 
+def pair_live(first, width, blocks):
+    slot = lax.broadcasted_iota(jnp.int32, (1, SLOTS * BLOCK), 1) // BLOCK
+    near = 2 * WMAX + 2
+    named = first + slot - WMAX
+    rows = []
+    for half in range(2):
+        offset = slot - WMAX - half
+        window = (slot < near) & (offset <= width) & (offset >= -width)
+        window = window & (named >= 0) & (named < blocks)
+        own = near + 2 + 2 * half
+        other = ((slot >= near) & (slot < near + 2)) | ((slot >= own) & (slot < own + 2))
+        rows.append(jnp.where(window | other, 1.0, 0.0).astype(f32))
+    return rows
+
+
 def greet(me, devices):
     barrier = pltpu.get_barrier_semaphore()
     for step in range(1, devices):
@@ -65,6 +79,14 @@
     pl.semaphore_wait(barrier, devices - 1)
 
 
+def partner(me, step, devices):
+    other, place = 0, 1
+    while place < devices:
+        other += lax.rem(me // place + step // place, 2) * place
+        place *= 2
+    return other
+
+
 def columns(head, head_dim):
     return pl.ds(pl.multiple_of(head * head_dim, head_dim), head_dim)
 
@@ -75,7 +97,7 @@
 
 def main_kernel(
     devices, group_size,
-    slots, live, q, k, v, dq, dk, dv,
+    widths, globals_, randoms, q, k, v, dq, dk, dv,
     q_gn, window, fixed, drawn,
     q_all, k_all, v_all, dq_all, dk_all, dv_all, q_res,
     send, recv, q_send, q_recv,
@@ -86,13 +108,14 @@
     head_dim = k_all.shape[2]
     own = tokens // group_size
     pairs = own // PAIR
+    blocks = local_blocks * devices
     head, residue = me // group_size, lax.rem(me, group_size)
     kinds = [(k, k_all), (dk, dk_all), (v, v_all), (dv, dv_all), (q, q_all), (dq, dq_all)]
     greet(me, devices)
 
     def copy(kind, step):
         source, target = kinds[kind]
-        to = lax.rem(me + (devices - step * STRIDE % devices), devices)
+        to = me if isinstance(step, int) and step == 0 else partner(me, step, devices)
         if kind < 4:
             part = source.at[:, :, columns(to // group_size, head_dim)]
             spot = target.at[rows_at(me, local_blocks)]
@@ -101,7 +124,7 @@
                 rows_at(lax.rem(to, group_size), own), columns(to // group_size, head_dim)
             ]
             spot = target.at[rows_at(me, own), :]
-        if step == 0:
+        if isinstance(step, int) and step == 0:
             return pltpu.make_async_copy(part, spot, recv.at[kind, 0])
         return pltpu.make_async_remote_copy(
             src_ref=part,
@@ -112,11 +135,29 @@
             device_id_type=MESH,
         )
 
-    for kind in range(6):
-        for step in range(devices):
+    half = devices // 2
+    order = list(range(half, devices)) + list(range(half))
+    for kind in range(4):
+        for step in order:
+            copy(kind, step).start()
+    for kind in (4, 5):
+        for step in range(half):
             copy(kind, step).start()
     window[...] = jnp.zeros_like(window)
     fixed[...] = jnp.zeros_like(fixed)
+    for step in range(half, devices):
+        copy(3, step).wait_send()
+        if step < half + FLIGHT:
+            for kind in (4, 5):
+                copy(kind, step).start()
+
+    def send_far(place):
+        @pl.when(place < half)
+        def _():
+            for kind in (4, 5):
+                copy(kind, half + place - FLIGHT).wait_send()
+                copy(kind, half + place).start()
+
     for kind in range(4):
         for step in range(devices):
             if step == 0:
@@ -140,19 +181,21 @@
         )
 
     def work(step):
-        origin = lax.rem(me + step * STRIDE, devices)
+        origin = partner(me, step, devices)
         for pair in range(pairs):
             index = origin * pairs + pair
             rows = rows_at(index, PAIR)
-            ids = [slots[index, s] for s in range(SLOTS)]
+            first = origin * local_blocks + residue * (own // BLOCK) + 2 * pair
+            ids = [jnp.clip(first + o, 0, blocks - 1) for o in range(-WMAX, WMAX + 2)]
+            ids += [globals_[2 * head + s] for s in range(2)]
+            ids += [randoms[2 * (head * blocks + first) + s] for s in range(4)]
             query_part, added = pair_product(
                 q_all[rows, :], dq_all[rows, :],
                 gather(k_all, ids), gather(v_all, ids),
                 gather(dk_all, ids), gather(dv_all, ids),
-                live[index],
+                pair_live(first, widths[head], blocks),
             )
             q_res[rows, :] = query_part
-            first = origin * (tokens // BLOCK) + residue * (own // BLOCK) + 2 * pair
             near = (2 * WMAX + 2) * BLOCK
             spot = pl.ds(pl.multiple_of(first * BLOCK, BLOCK), near)
             window[spot, :] += added[:near]
@@ -167,33 +210,53 @@
     )
     copy(4, 0).wait()
     copy(5, 0).wait()
-    work(0)
-    own_copy.start()
-
-    def wait_rows(kind, step):
-        source, target = kinds[kind]
-        pltpu.make_async_remote_copy(
-            src_ref=source.at[rows_at(residue, own), columns(head, head_dim)],
-            dst_ref=target.at[rows_at(lax.rem(me + step * STRIDE, devices), own), :],
-            send_sem=send.at[kind, step],
-            recv_sem=recv.at[kind, step],
-            device_id={"seq": lax.rem(me + step * STRIDE, devices)},
-            device_id_type=MESH,
-        ).wait_recv()
-
-    @pl.loop(1, devices)
+
+    def wait_rows(step):
+        origin = partner(me, step, devices)
+        for kind in (4, 5):
+            source, target = kinds[kind]
+            pltpu.make_async_remote_copy(
+                src_ref=source.at[rows_at(residue, own), columns(head, head_dim)],
+                dst_ref=target.at[rows_at(origin, own), :],
+                send_sem=send.at[kind, step],
+                recv_sem=recv.at[kind, step],
+                device_id={"seq": origin},
+                device_id_type=MESH,
+            ).wait_recv()
+
+    @pl.loop(0, half)
     def _(step):
-        wait_rows(4, step)
-        wait_rows(5, step)
+        @pl.when(step > 0)
+        def _():
+            wait_rows(step)
+
         origin = work(step)
-        back(step, origin).start()
+
+        @pl.when(step > 0)
+        def _():
+            back(step, origin).start()
+
+        @pl.when(step == 0)
+        def _():
+            own_copy.start()
+
+        @pl.when(lax.rem(step, 2) == 1)
+        def _():
+            send_far(FLIGHT + step // 2)
+
+    @pl.loop(half, devices)
+    def _(step):
+        send_far(FLIGHT + half // 2 + step - half)
+        wait_rows(step)
+        back(step, work(step)).start()
 
     for kind in range(6):
         for step in range(1, devices):
-            copy(kind, step).wait_send()
+            if step < half or kind in (0, 1, 2) or (kind > 3 and step >= devices - FLIGHT):
+                copy(kind, step).wait_send()
     own_copy.wait()
     for step in range(1, devices):
-        giver = lax.rem(me + (devices - step * STRIDE % devices), devices)
+        giver = partner(me, step, devices)
         pltpu.make_async_remote_copy(
             src_ref=q_res.at[rows_at(giver, own), :],
             dst_ref=q_gn.at[
@@ -207,17 +270,23 @@
         ).wait()
 
 
-def add_kernel(slots, window, fixed, drawn, k_out, v_out, acc):
+def add_kernel(group_size, local_blocks, globals_, randoms, window, fixed, drawn, k_out, v_out, acc):
     tokens, head_dim = k_out.shape
+    blocks = tokens // BLOCK
+    me = lax.axis_index("seq")
+    head, residue = me // group_size, lax.rem(me, group_size)
+    own_blocks = local_blocks // group_size
+    pairs = own_blocks // 2
     acc[...] = window[pl.ds(WMAX * BLOCK, tokens), :]
     for s in range(2):
-        rows = rows_at(slots[0, 2 * WMAX + 2 + s], BLOCK)
+        rows = rows_at(globals_[2 * head + s], BLOCK)
         acc[rows, :] += fixed[s * BLOCK : (s + 1) * BLOCK, :]
 
-    @pl.loop(0, slots.shape[0])
+    @pl.loop(0, drawn.shape[0] // (4 * BLOCK))
     def _(index):
+        first = index // pairs * local_blocks + residue * own_blocks + 2 * lax.rem(index, pairs)
         for s in range(4):
-            rows = rows_at(slots[index, 2 * WMAX + 4 + s], BLOCK)
+            rows = rows_at(randoms[2 * (head * blocks + first) + s], BLOCK)
             acc[rows, :] += drawn[rows_at(index * 4 + s, BLOCK), :].astype(f32)
 
     k_out[...] = acc[:, :head_dim].astype(bf16)
@@ -231,10 +300,10 @@
 
     def copy(kind, step):
         source, target = ((k, k_gn), (v, v_gn))[kind]
-        to = lax.rem(me + step * STRIDE, devices)
+        to = partner(me, step, devices)
         part = source.at[rows_at(to, tokens), :]
         spot = target.at[lax.rem(me, group_size), :, columns(me // group_size, head_dim)]
-        if step == 0:
+        if isinstance(step, int) and step == 0:
             return pltpu.make_async_copy(part, spot, recv.at[kind, 0])
         return pltpu.make_async_remote_copy(
             src_ref=part,
@@ -245,41 +314,13 @@
             device_id_type=MESH,
         )
 
-    for kind in range(2):
-        for step in range(devices):
+    half = devices // 2
+    for step in list(range(half, devices)) + list(range(half)):
+        for kind in range(2):
             copy(kind, step).start()
     for kind in range(2):
         for step in range(devices):
             copy(kind, step).wait()
-
-
-def pair_slots(first_ids, head_window, head_globals, head_randoms, block_count):
-    count = first_ids.shape[0]
-    offsets = jnp.arange(-WMAX, WMAX + 2, dtype=jnp.int32)
-    named = first_ids[:, None] + offsets[None, :]
-    inside = (named >= 0) & (named < block_count)
-    halves = [
-        inside & (jnp.abs(offsets - half)[None, :] <= head_window) for half in range(2)
-    ]
-    ones = jnp.ones((count, 2), bool)
-    none = jnp.zeros((count, 2), bool)
-    ids = jnp.concatenate(
-        [
-            jnp.clip(named, 0, block_count - 1),
-            jnp.broadcast_to(head_globals[None, :], (count, 2)),
-            head_randoms[first_ids],
-            head_randoms[first_ids + 1],
-        ],
-        axis=1,
-    )
-    live = jnp.stack(
-        [
-            jnp.concatenate([halves[0], ones, ones, none], axis=1),
-            jnp.concatenate([halves[1], ones, none, ones], axis=1),
-        ],
-        axis=1,
-    )
-    return ids, jnp.repeat(live.astype(f32), BLOCK, axis=2)
 
 
 def shards(
@@ -288,9 +329,6 @@
     devices = lax.axis_size("seq")
     head_count = window_width.shape[0]
     group_size = devices // head_count
-    device_index = lax.axis_index("seq")
-    head_id = device_index // group_size
-    residue = device_index % group_size
     tokens, features = queries.shape
     head_dim = features // head_count
     local_blocks = tokens // BLOCK
@@ -298,21 +336,13 @@
     own = own_blocks * BLOCK
     block_count = local_blocks * devices
     whole = devices * tokens
-    counter = 2 * jnp.arange(devices * own_blocks // 2, dtype=jnp.int32)
-    first_ids = counter // own_blocks * local_blocks + residue * own_blocks + counter % own_blocks
-    slots, live = pair_slots(
-        first_ids,
-        window_width[head_id],
-        global_blocks[head_id],
-        random_blocks[head_id],
-        block_count,
-    )
     by_block = lambda array: array.reshape(local_blocks, BLOCK, features)
     any_spec = pl.BlockSpec(memory_space=pl.ANY)
     vmem = pl.BlockSpec(memory_space=pltpu.VMEM)
     smem = pl.BlockSpec(memory_space=pltpu.SMEM)
     limit = 56 * 1024 * 1024
-    count = slots.shape[0]
+    count = devices * own_blocks // 2
+    named = (global_blocks.reshape(-1), random_blocks.reshape(-1))
     shape = jax.ShapeDtypeStruct
     rows, mine = pltpu.VMEM((block_count, BLOCK, head_dim), bf16), pltpu.VMEM((devices * own, head_dim), bf16)
     dma = pltpu.SemaphoreType.DMA
@@ -324,7 +354,7 @@
             shape((2 * BLOCK, 2 * head_dim), f32),
             shape((count * 4 * BLOCK, 2 * head_dim), bf16),
         ],
-        in_specs=[smem, vmem] + [any_spec] * 6,
+        in_specs=[smem] * 3 + [any_spec] * 6,
         out_specs=[any_spec, vmem, vmem, vmem],
         scratch_shapes=[
             mine, rows, rows, mine, rows, rows, mine,
@@ -334,17 +364,17 @@
             collective_id=0, has_side_effects=True, vmem_limit_bytes=limit
         ),
     )(
-        slots, live, queries, by_block(keys), by_block(values),
+        window_width, *named, queries, by_block(keys), by_block(values),
         query_dir, by_block(key_dir), by_block(value_dir),
     )
     key_grad, value_grad = pl.pallas_call(
-        add_kernel,
+        functools.partial(add_kernel, group_size, local_blocks),
         out_shape=[shape((whole, head_dim), bf16)] * 2,
-        in_specs=[smem, vmem, vmem, vmem],
+        in_specs=[smem, smem, vmem, vmem, vmem],
         out_specs=[vmem, vmem],
         scratch_shapes=[pltpu.VMEM((whole, 2 * head_dim), f32)],
         compiler_params=pltpu.CompilerParams(vmem_limit_bytes=limit),
-    )(slots, window, fixed, drawn)
+    )(*named, window, fixed, drawn)
     key_gn, value_gn = pl.pallas_call(
         functools.partial(return_kernel, devices, group_size),
         out_shape=[shape((group_size, tokens, features), bf16)] * 2,

time: 254 us -> 240 us (0.945)
  Pallas kernels: 240 us -> 231 us
    pallas_call x1, Pallas kernels: 180 us -> 172 us  [shards(): pl.pallas_call(functools.partial(main_kernel, devices, group_size), out_s...]
where the time goes in v2:
time: 240 us; the launch traced here: 239 us
  Pallas kernels  231 us (96%)
  local copies, waits for them, and re-layouts  7.51 us (3%)
    pallas_call x1, Pallas kernels, shards(): pl.pallas_call(functools.partial(main_kernel, devices, group_size), out_s...  172 us
    pallas_call x1, Pallas kernels, shards(): pl.pallas_call(functools.partial(return_kernel, devices, group_size), out...  52.3 us
    pallas_call x1, Pallas kernels, shards(): pl.pallas_call(functools.partial(add_kernel, group_size, local_blocks), o...  6.71 us
    unnamed x9, local copies, waits for them, and re-layouts  5.96 us

profile of v2, /device:TPU:9, one launch (start us, length us, event | category | flops | bytes accessed | tf_op | source)
XLA Modules:
  0.0 239.2 jit_solution(18124142623289345120)
XLA Ops:
  0.6 0.8 copy.13
  1.4 0.7 reshape.24.globals_
  2.1 0.9 copy.14
  3.0 0.9 reshape.25.randoms
  3.9 172.0 %shard_map.112 = (bf16[256,2048]{1,0:T(8,128)(2,1)}, f32[4352,256]{1,0:T(8,128)}, f32[128,256]{1,0:T(8,128)}, bf16[8192,256]{1,0:T(8,128)(2,1)}) custom-call(s32[16]{0:T(128)} %widths.1, s32[32]{0:T(128)} %reshape.24.globals_, s32[2048]{0:T(1024)} %reshape.25.randoms, bf16[256,2048]{1,0:T(8,128)(2,1)} %q.1, bf16[4,64,2048]{2,1,0:T(8,128)(2,1)} %bitcast.8, ...), custom_call_target="tpu_custom_call" | custom-call | tf_op jit(solution)/shard_map/pallas_call | solution.py:349
  175.9 0.0 copy-start
  175.9 6.7 %shard_map.113 = (bf16[4096,128]{1,0:T(8,128)(2,1)}, bf16[4096,128]{1,0:T(8,128)(2,1)}) custom-call(s32[32]{0:T(128)} %reshape.24.globals_, s32[2048]{0:T(1024)} %reshape.25.randoms, f32[4352,256]{1,0:T(8,128)} %get-tuple-element.12.window, f32[128,256]{1,0:T(8,128)} %get-tuple-element.13.fixed, bf16[8192,256]{1,0:T(8,128)(2,1)} %get-tuple-element.14.drawn), custom_call_target="tpu_custom_call" | custom-call | tf_op jit(solution)/shard_map/pallas_call | solution.py:370
  182.6 52.3 %shard_map.114 = (bf16[1,256,2048]{2,1,0:T(8,128)(2,1)}, bf16[1,256,2048]{2,1,0:T(8,128)(2,1)}) custom-call(bf16[4096,128]{1,0:T(8,128)(2,1)} %get-tuple-element.15.k, bf16[4096,128]{1,0:T(8,128)(2,1)} %get-tuple-element.16.v), custom_call_target="tpu_custom_call" | custom-call | tf_op jit(solution)/shard_map/pallas_call | solution.py:378
  234.9 0.0 copy-start.1
  234.9 0.0 copy-done
  235.0 1.0 copy.18
  235.9 2.3 copy.19
  238.2 0.0 copy-done.1
  238.2 1.0 copy.20
Async XLA Ops:
  175.9 59.0 %copy-start = (bf16[256,2048]{1,0:T(8,128)(2,1)S(1)}, bf16[256,2048]{1,0:T(8,128)(2,1)}, u32[]{:S(2)}) copy-start(bf16[256,2048]{1,0:T(8,128)(2,1)} %get-tuple-element.22) | copy-start | bytes 3145732
  234.9 3.3 %copy-start.1 = (bf16[1,256,2048]{2,1,0:T(8,128)(2,1)S(1)}, bf16[1,256,2048]{2,1,0:T(8,128)(2,1)}, u32[]{:S(2)}) copy-start(bf16[1,256,2048]{2,1,0:T(8,128)(2,1)} %get-tuple-element.18) | copy-start | bytes 3145732

commit v3 on v2

--- a/solution.py
+++ b/solution.py
@@ -136,7 +136,7 @@
         )
 
     half = devices // 2
-    order = list(range(half, devices)) + list(range(half))
+    order = [step for near in range(half) for step in (half + near, near)]
     for kind in range(4):
         for step in order:
             copy(kind, step).start()
@@ -315,7 +315,7 @@
         )
 
     half = devices // 2
-    for step in list(range(half, devices)) + list(range(half)):
+    for step in [step for near in range(half) for step in (half + near, near)]:
         for kind in range(2):
             copy(kind, step).start()
     for kind in range(2):

time: 240 us -> 236 us (0.983)
  Pallas kernels: 231 us -> 227 us
    pallas_call x1, Pallas kernels: 172 us -> 170 us  [shards(): pl.pallas_call(functools.partial(main_kernel, devices, group_size), out_s...]
where the time goes in v3:
time: 236 us; the launch traced here: 235 us
  Pallas kernels  227 us (96%)
  local copies, waits for them, and re-layouts  7.51 us (3%)
    pallas_call x1, Pallas kernels, shards(): pl.pallas_call(functools.partial(main_kernel, devices, group_size), out_s...  170 us
    pallas_call x1, Pallas kernels, shards(): pl.pallas_call(functools.partial(return_kernel, devices, group_size), out...  50.9 us
    pallas_call x1, Pallas kernels, shards(): pl.pallas_call(functools.partial(add_kernel, group_size, local_blocks), o...  6.71 us
    unnamed x9, local copies, waits for them, and re-layouts  5.96 us

profile of v3, /device:TPU:9, one launch (start us, length us, event | category | flops | bytes accessed | tf_op | source)
XLA Modules:
  0.0 235.4 jit_solution(14309517445720425279)
XLA Ops:
  0.6 0.8 copy.13
  1.4 0.7 reshape.24.globals_
  2.1 0.9 copy.14
  3.0 0.9 reshape.25.randoms
  3.9 169.6 %shard_map.112 = (bf16[256,2048]{1,0:T(8,128)(2,1)}, f32[4352,256]{1,0:T(8,128)}, f32[128,256]{1,0:T(8,128)}, bf16[8192,256]{1,0:T(8,128)(2,1)}) custom-call(s32[16]{0:T(128)} %widths.1, s32[32]{0:T(128)} %reshape.24.globals_, s32[2048]{0:T(1024)} %reshape.25.randoms, bf16[256,2048]{1,0:T(8,128)(2,1)} %q.1, bf16[4,64,2048]{2,1,0:T(8,128)(2,1)} %bitcast.8, ...), custom_call_target="tpu_custom_call" | custom-call | tf_op jit(solution)/shard_map/pallas_call | solution.py:349
  173.5 0.0 copy-start
  173.5 6.7 %shard_map.113 = (bf16[4096,128]{1,0:T(8,128)(2,1)}, bf16[4096,128]{1,0:T(8,128)(2,1)}) custom-call(s32[32]{0:T(128)} %reshape.24.globals_, s32[2048]{0:T(1024)} %reshape.25.randoms, f32[4352,256]{1,0:T(8,128)} %get-tuple-element.12.window, f32[128,256]{1,0:T(8,128)} %get-tuple-element.13.fixed, bf16[8192,256]{1,0:T(8,128)(2,1)} %get-tuple-element.14.drawn), custom_call_target="tpu_custom_call" | custom-call | tf_op jit(solution)/shard_map/pallas_call | solution.py:370
  180.2 50.9 %shard_map.114 = (bf16[1,256,2048]{2,1,0:T(8,128)(2,1)}, bf16[1,256,2048]{2,1,0:T(8,128)(2,1)}) custom-call(bf16[4096,128]{1,0:T(8,128)(2,1)} %get-tuple-element.15.k, bf16[4096,128]{1,0:T(8,128)(2,1)} %get-tuple-element.16.v), custom_call_target="tpu_custom_call" | custom-call | tf_op jit(solution)/shard_map/pallas_call | solution.py:378
  231.2 0.0 copy-start.1
  231.2 0.0 copy-done
  231.2 1.0 copy.18
  232.2 2.3 copy.19
  234.5 0.0 copy-done.1
  234.5 1.0 copy.20
Async XLA Ops:
  173.5 57.7 %copy-start = (bf16[256,2048]{1,0:T(8,128)(2,1)S(1)}, bf16[256,2048]{1,0:T(8,128)(2,1)}, u32[]{:S(2)}) copy-start(bf16[256,2048]{1,0:T(8,128)(2,1)} %get-tuple-element.22) | copy-start | bytes 3145732
  231.2 3.3 %copy-start.1 = (bf16[1,256,2048]{2,1,0:T(8,128)(2,1)S(1)}, bf16[1,256,2048]{2,1,0:T(8,128)(2,1)}, u32[]{:S(2)}) copy-start(bf16[1,256,2048]{2,1,0:T(8,128)(2,1)} %get-tuple-element.18) | copy-start | bytes 3145732
